TPU v7x, 32 devices: a whole 2x2x4 slice. The times are simulated.
32 devices in a mesh: group: 2 (over y), fsdp: 2 (over core), tensor: 8 (over z, x).
Axes of the slice: x: 2, y: 2, z: 4, core: 2. Of those that a mesh axis runs over, the one named last changes fastest.
Arguments:
- step_token_rows: int32 [4, 4], P('group'), parts along dimension 0, may hold values from 0 to 9599
- token_embedding_table: bfloat16 [9600, 5120], P(('fsdp', 'tensor')), may hold values from -3 to 3
- cached_row_lengths: int32 [4], P(('group', 'fsdp')), parts along dimension 0, may hold values from 1024 to 4096, as said below
- key_value_cache: bfloat16 [4, 4096, 2048], P(('group', 'fsdp'), 'tensor'), parts along dimension 0, may hold values from -120 to 120, as said below
- input_norm_gain: bfloat16 [5120], replicated, may hold values from 0.5 to 1.5
- query_key_gains: float32 [2, 128], replicated, may hold values from 1.2 to 2.5
- wqkv: bfloat16 [5120, 10240], P('tensor'), may hold values from -0.078125 to 0.078125
- wout: bfloat16 [8192, 5120], P('tensor'), may hold values from -0.0625 to 0.0625
- adapter_down_projections: bfloat16 [5120, 384], P('tensor'), may hold values from -0.078125 to 0.078125
- adapter_down_output: bfloat16 [8192, 128], P('tensor'), may hold values from -0.0625 to 0.0625
- adapter_up_factors: bfloat16 [128, 15360], P(None, ('fsdp', 'tensor')), may hold values from -0.25 to 0.25
Outputs:
- hidden_out: bfloat16 [4, 4, 5120], P(('group', 'fsdp')), parts along dimension 0
There are 2 independent parts, one for each index of `group`. A program takes and returns all parts, laid end to end along the dimension named above; an argument that names none is the same for every part. Nothing has to cross between parts.
Inputs may be any that keep to these rules, and one draw needn't show every extreme that they name: Row b's cache holds valid entries at its first cached_row_lengths[b] positions only; in every draw some row holds all 4096. `key_value_cache`: entries at positions at or after a row's length are not read.
All inputs are finite; a program needn't handle non-finite values.
Results may differ from a plain program's by a relative error of at most 0.035.
Values may be sent and summed in bfloat16 or wider, within the bound.
A program may use at most 192 MiB of HBM per device.

v0:
```python
import math

import jax
import jax.numpy as jnp
from jax import lax
from jax.sharding import PartitionSpec as P

QUERY_HEADS = 64
KVH = 8
HEAD_SIZE = 128
ADAPTER_RANK = 128
STEPS = 4


EPSILON = 1e-06
ROPE_BASE = 1000000.0
ADAPTER_SCALE = 2.0


def combined_all(x, axis, join):
    gathered = jax.tree.map(
        lambda a, kind: lax.all_gather(a.astype(kind), axis),
        x,
        (jnp.bfloat16, jnp.bfloat16, jnp.bfloat16),
    )

    def take(source):
        return jax.tree.map(
            lambda a, own: lax.dynamic_index_in_dim(a, source, 0, False).astype(own.dtype),
            gathered,
            x,
        )

    return lax.fori_loop(
        1, lax.axis_size(axis), lambda source, state: join(state, take(source)), take(0)
    )


def rms_scale(values, gain):
    return values * lax.rsqrt(jnp.mean(values * values, axis=-1, keepdims=True) + EPSILON) * gain


def rotate(values, position):
    half_width = values.shape[-1] // 2
    inverse = ROPE_BASE ** (-(2.0 * jnp.arange(half_width, dtype=jnp.float32)) / values.shape[-1])
    angle = position[..., None] * inverse
    cosine = jnp.cos(angle)
    sine = jnp.sin(angle)
    first_half = values[..., :half_width]
    second_half = values[..., half_width:]
    return jnp.concatenate(
        [first_half * cosine - second_half * sine, second_half * cosine + first_half * sine],
        axis=-1,
    )


def fold_parts(earlier, later):
    top = jnp.maximum(earlier[0], later[0])
    scale_one = jnp.exp(earlier[0] - top)
    scale_two = jnp.exp(later[0] - top)
    return (
        top,
        earlier[1] * scale_one + later[1] * scale_two,
        earlier[2] * scale_one[..., None] + later[2] * scale_two[..., None],
    )


def local(
    step_token_rows,
    token_embedding_table,
    cached_row_lengths,
    key_value_cache,
    input_norm_gain,
    query_key_gains,
    wqkv,
    wout,
    adapter_down_projections,
    adapter_down_output,
    adapter_up_factors,
):
    tensor_count = lax.axis_size("tensor")
    tensor_index = lax.axis_index("tensor")
    fsdp_index = lax.axis_index("fsdp")
    rows_here = cached_row_lengths.shape[0]
    heads_here = QUERY_HEADS // tensor_count
    slots_here = key_value_cache.shape[1]
    groups = QUERY_HEADS // KVH
    query_width = QUERY_HEADS * HEAD_SIZE
    key_value_width = KVH * HEAD_SIZE
    projection_width = wqkv.shape[1]
    model_width = token_embedding_table.shape[1]
    scaling = 1.0 / math.sqrt(HEAD_SIZE)
    adapter_up_whole = lax.all_gather(adapter_up_factors, ("fsdp", "tensor"), axis=1, tiled=True)
    weight_delta = jnp.concatenate(
        [
            jnp.dot(
                adapter_down_projections[:, :ADAPTER_RANK],
                adapter_up_whole[:, :query_width],
                preferred_element_type=jnp.float32,
            ),
            jnp.dot(
                adapter_down_projections[:, ADAPTER_RANK : 2 * ADAPTER_RANK],
                adapter_up_whole[:, query_width : query_width + key_value_width],
                preferred_element_type=jnp.float32,
            ),
            jnp.dot(
                adapter_down_projections[:, 2 * ADAPTER_RANK :],
                adapter_up_whole[:, query_width + key_value_width : projection_width],
                preferred_element_type=jnp.float32,
            ),
        ],
        axis=1,
    )
    merged_projection_weight = (wqkv.astype(jnp.float32) + ADAPTER_SCALE * weight_delta).astype(
        jnp.bfloat16
    )
    output_weight_delta = jnp.dot(
        adapter_down_output,
        adapter_up_whole[:, projection_width:],
        preferred_element_type=jnp.float32,
    )
    merged_output_weight = (wout.astype(jnp.float32) + ADAPTER_SCALE * output_weight_delta).astype(
        jnp.bfloat16
    )
    shard_rows = token_embedding_table.shape[0]
    first_row = (fsdp_index * tensor_count + tensor_index) * shard_rows
    flat_ids = step_token_rows.reshape(-1)
    one_hot = (
        flat_ids[:, None] == first_row + jnp.arange(shard_rows, dtype=jnp.int32)[None, :]
    ).astype(jnp.bfloat16)
    lookup_terms = jnp.dot(one_hot, token_embedding_table, preferred_element_type=jnp.float32)
    looked_up = lax.psum(lookup_terms, ("fsdp", "tensor"))
    embedded = lax.dynamic_slice_in_dim(
        looked_up.reshape(-1, STEPS, model_width), fsdp_index * rows_here, rows_here, 0
    )
    in_rows = wqkv.shape[0]
    cache_keys = key_value_cache[:, :, :key_value_width].reshape(
        rows_here, slots_here, KVH, HEAD_SIZE
    )
    cache_values = key_value_cache[:, :, key_value_width:].reshape(
        rows_here, slots_here, KVH, HEAD_SIZE
    )
    global_slot = tensor_index * slots_here + jnp.arange(slots_here, dtype=jnp.int32)
    visible = global_slot[None, :] < cached_row_lengths[:, None]
    visible_grid = visible[:, None, None, :]

    def own_heads(array):
        return lax.dynamic_slice_in_dim(array, tensor_index * heads_here, heads_here, 1)

    key_list = []
    value_list = []
    results = []
    for decode_step in range(STEPS):
        inputs = embedded[:, decode_step]
        normed = rms_scale(inputs, input_norm_gain.astype(jnp.float32)).astype(jnp.bfloat16)
        normed_slice = lax.dynamic_slice_in_dim(normed, tensor_index * in_rows, in_rows, 1)
        partial_qkv = jnp.dot(
            normed_slice, merged_projection_weight, preferred_element_type=jnp.float32
        )
        projected = lax.psum(partial_qkv, "tensor").astype(jnp.bfloat16)
        queries = (
            projected[:, :query_width]
            .astype(jnp.float32)
            .reshape(rows_here, QUERY_HEADS, HEAD_SIZE)
        )
        new_key = (
            projected[:, query_width : query_width + key_value_width]
            .astype(jnp.float32)
            .reshape(rows_here, KVH, HEAD_SIZE)
        )
        new_value = projected[:, query_width + key_value_width :].reshape(rows_here, KVH, HEAD_SIZE)
        position = (cached_row_lengths + decode_step).astype(jnp.float32)[:, None]
        rotated_query = rotate(rms_scale(queries, query_key_gains[0]), position).astype(
            jnp.bfloat16
        )
        key_list.append(
            rotate(rms_scale(new_key, query_key_gains[1]), position).astype(jnp.bfloat16)
        )
        value_list.append(new_value)
        query_grid = rotated_query.reshape(rows_here, KVH, groups, HEAD_SIZE)
        scores = (
            jnp.einsum(
                "bgrd,bjgd->bgrj", query_grid, cache_keys, preferred_element_type=jnp.float32
            )
            * scaling
        )
        local_max = jnp.max(jnp.where(visible_grid, scores, -1e30), axis=-1)
        weights = jnp.where(visible_grid, jnp.exp(scores - local_max[..., None]), 0.0)
        local_sum = jnp.sum(weights, axis=-1)
        local_acc = jnp.einsum(
            "bgrj,bjgd->bgrd",
            weights.astype(jnp.bfloat16),
            cache_values,
            preferred_element_type=jnp.float32,
        )
        local_max = local_max.reshape(rows_here, QUERY_HEADS)
        local_sum = local_sum.reshape(rows_here, QUERY_HEADS)
        local_acc = local_acc.reshape(rows_here, QUERY_HEADS, HEAD_SIZE)
        merged_parts = combined_all((local_max, local_sum, local_acc), "tensor", fold_parts)
        cache_part = (
            own_heads(merged_parts[0]),
            own_heads(merged_parts[1]),
            own_heads(merged_parts[2]),
        )
        stacked_keys = jnp.stack(key_list, axis=1)
        stacked_values = jnp.stack(value_list, axis=1)
        fresh_scores = (
            jnp.einsum(
                "bgrd,bsgd->bgrs", query_grid, stacked_keys, preferred_element_type=jnp.float32
            )
            * scaling
        )
        fresh_max = jnp.max(fresh_scores, axis=-1)
        fresh_weights = jnp.exp(fresh_scores - fresh_max[..., None])
        fresh_sum = jnp.sum(fresh_weights, axis=-1)
        fresh_acc = jnp.einsum(
            "bgrs,bsgd->bgrd",
            fresh_weights.astype(jnp.bfloat16),
            stacked_values,
            preferred_element_type=jnp.float32,
        )
        fresh_part = (
            own_heads(fresh_max.reshape(rows_here, QUERY_HEADS)),
            own_heads(fresh_sum.reshape(rows_here, QUERY_HEADS)),
            own_heads(fresh_acc.reshape(rows_here, QUERY_HEADS, HEAD_SIZE)),
        )
        combined = fold_parts(cache_part, fresh_part)
        attended = (
            (combined[2] / combined[1][..., None])
            .reshape(rows_here, heads_here * HEAD_SIZE)
            .astype(jnp.bfloat16)
        )
        partial_out = jnp.dot(attended, merged_output_weight, preferred_element_type=jnp.float32)
        summed_out = lax.psum(partial_out, "tensor")
        results.append((inputs + summed_out).astype(jnp.bfloat16))
    return jnp.stack(results, axis=1)


def solution(mesh):
    in_specs = (
        P("group", None),
        P(("fsdp", "tensor"), None),
        P(("group", "fsdp")),
        P(("group", "fsdp"), "tensor", None),
        P(),
        P(),
        P("tensor", None),
        P("tensor", None),
        P("tensor", None),
        P("tensor", None),
        P(None, ("fsdp", "tensor")),
    )
    out_specs = P(("group", "fsdp"), None, None)
    return jax.shard_map(local, mesh=mesh, in_specs=in_specs, out_specs=out_specs, check_vma=False)
```

profile of v0, /device:TPU:0, one launch (start us, length us, event | category | flops | bytes accessed | tf_op | source)
XLA Modules:
  0.0 659.4 jit_solution(203936346101896523)
XLA Ops:
  6.5 0.8 eq.15
  7.4 3.8 fusion.92
  11.1 0.7 reshape.2274
  11.9 0.7 all-gather.2.cloned.1.call-update
  12.7 0.7 convert_element_type.812
  14.0 1.7 fusion.257
  15.7 0.5 copy.204
  16.3 0.5 copy.205
  17.1 85.3 %all-reduce.6.cloned.1.call-done = f32[2,4,5120]{2,1,0:T(4,128)} async-done(((f32[2,4,5120]{2,1,0:T(4,128)}), f32[2,4,5120]{2,1,0:T(4,128)}) %all-reduce.6.cloned.1.call-update) | async-done | bytes 163856 | tf_op jit(solution)/shard_map/psum | solution.py:132
  102.4 1.8 fusion.89
  106.8 1.2 broadcast_multiply_fusion
  108.1 46.3 %all-gather.2.cloned.1.call-done = bf16[128,15360]{0,1:T(8,128)(2,1)} async-done(((bf16[128,960]{0,1:T(8,128)(2,1)}), bf16[128,15360]{0,1:T(8,128)(2,1)}) %all-gather.2.cloned.1.call-update) | async-done | bytes 3932176 | tf_op jit(solution)/shard_map/all_gather | solution.py:93
  154.4 11.6 %fusion.42 = f32[640,8192]{1,0:T(8,128)} fusion(bf16[128,15360]{0,1:T(8,128)(2,1)} %all-gather.2.cloned.1.call-done, bf16[640,384]{1,0:T(8,128)(2,1)} %param.27), kind=kOutput, calls=%fused_computation.64 | convolution fusion | flops 1342177280 | bytes 23232512 | tf_op jit(solution)/shard_map/dot_general | solution.py:96
  166.0 2.9 fusion.49
  168.9 3.0 fusion.51
  171.9 18.4 %fusion.41 = bf16[640,10240]{1,0:T(8,128)(2,1)} fusion(f32[640,1024]{1,0:T(8,128)} %fusion.49, f32[640,1024]{1,0:T(8,128)} %fusion.51, f32[640,8192]{1,0:T(8,128)} %fusion.42, bf16[640,10240]{1,0:T(8,128)(2,1)} %param.25), kind=kLoop, calls=%fused_computation.62 | loop fusion | flops 39321600 | bytes 52428800 | tf_op jit(solution)/shard_map/convert_element_type | solution.py:114
  190.3 6.7 %fusion.263 = f32[1,10240]{1,0:T(1,128)S(1)} fusion(bf16[640,1]{0,1:T(2,128)(2,1)S(1)} %reshape.2359, bf16[640,10240]{1,0:T(8,128)(2,1)} %fusion.41), kind=kOutput, calls=%fused_computation.437 | convolution fusion | flops 13107200 | bytes 13149440 | tf_op jit(solution)/shard_map/dot_general | solution.py:157
  196.9 1.8 copy-done.2
  198.7 1.8 fusion.265
  200.5 1.8 fusion.267
  202.3 1.8 fusion.261
  204.1 74.4 %all-reduce.9 = (bf16[1,10240]{1,0:T(2,128)(2,1)S(1)}, bf16[1,10240]{1,0:T(2,128)(2,1)S(1)}, bf16[1,10240]{1,0:T(2,128)(2,1)S(1)}, bf16[1,10240]{1,0:T(2,128)(2,1)S(1)}) all-reduce(f32[1,10240]{1,0:T(1,128)S(1)} %fusion.261, f32[1,10240]{1,0:T(1,128)S(1)} %fusion.263, ...), channel_id=1, replica_groups=mesh['group'=2,'fsdp'=2,'tensor'=8] {'tensor'}, use_global_device_ids=true, to_apply=%region_2.0 | all-reduce | flops 40960 | bytes 245760 | tf_op jit(solution)/shard_map/psum | solution.py:160
  279.8 0.4 fusion.45
  284.0 30.5 %all_gather.54 = bf16[8,1,64,128]{3,2,1,0:T(8,128)(2,1)S(1)} all-gather(bf16[1,1,64,128]{3,2,1,0:T(8,128)(2,1)S(1)} %fusion.45), channel_id=1, replica_groups=mesh['group'=2,'fsdp'=2,'tensor'=8] {'tensor'}, dimensions={0}, use_global_device_ids=true | all-gather | bytes 147456 | tf_op jit(solution)/shard_map/all_gather | solution.py:22
  314.6 19.8 %all_gather.53 = bf16[8,1,64]{2,1,0:T(2,128)(2,1)S(1)} all-gather(bf16[1,1,64]{2,1,0:T(2,128)(2,1)S(1)} %convert_element_type.823), channel_id=1, replica_groups=mesh['group'=2,'fsdp'=2,'tensor'=8] {'tensor'}, dimensions={0}, use_global_device_ids=true | all-gather | bytes 1152 | tf_op jit(solution)/shard_map/all_gather | solution.py:22
  334.5 16.2 %all_gather.52 = bf16[8,1,64]{2,1,0:T(2,128)(2,1)S(1)} all-gather(bf16[1,1,64]{2,1,0:T(2,128)(2,1)S(1)} %convert_element_type.819), channel_id=1, replica_groups=mesh['group'=2,'fsdp'=2,'tensor'=8] {'tensor'}, dimensions={0}, use_global_device_ids=true | all-gather | bytes 1152 | tf_op jit(solution)/shard_map/all_gather | solution.py:22
  350.7 1.2 while.76
  352.4 30.5 %all_gather.57 = bf16[8,1,64,128]{3,2,1,0:T(8,128)(2,1)S(1)} all-gather(bf16[1,1,64,128]{3,2,1,0:T(8,128)(2,1)S(1)} %fusion.46), channel_id=1, replica_groups=mesh['group'=2,'fsdp'=2,'tensor'=8] {'tensor'}, dimensions={0}, use_global_device_ids=true | all-gather | bytes 147456 | tf_op jit(solution)/shard_map/all_gather | solution.py:22
  383.0 18.2 %all_gather.56 = bf16[8,1,64]{2,1,0:T(2,128)(2,1)S(1)} all-gather(bf16[1,1,64]{2,1,0:T(2,128)(2,1)S(1)} %convert_element_type.845), channel_id=1, replica_groups=mesh['group'=2,'fsdp'=2,'tensor'=8] {'tensor'}, dimensions={0}, use_global_device_ids=true | all-gather | bytes 1152 | tf_op jit(solution)/shard_map/all_gather | solution.py:22
  401.3 16.2 %all_gather.55 = bf16[8,1,64]{2,1,0:T(2,128)(2,1)S(1)} all-gather(bf16[1,1,64]{2,1,0:T(2,128)(2,1)S(1)} %convert_element_type.841), channel_id=1, replica_groups=mesh['group'=2,'fsdp'=2,'tensor'=8] {'tensor'}, dimensions={0}, use_global_device_ids=true | all-gather | bytes 1152 | tf_op jit(solution)/shard_map/all_gather | solution.py:22
  417.4 1.2 while.77
  419.4 8.4 %add_convert_fusion = bf16[1024,5120]{1,0:T(8,128)(2,1)} fusion(bf16[1024,5120]{1,0:T(8,128)(2,1)} %param.26, bf16[1024,128]{1,0:T(8,128)(2,1)S(1)} %copy-done, bf16[128,15360]{0,1:T(8,128)(2,1)} %all-gather.2.cloned.1.call-done), kind=kOutput, calls=%fused_computation.63 | convolution fusion | flops 1363148800 | bytes 22544384 | tf_op jit(solution)/shard_map/dot_general | solution.py:117
  427.8 6.2 fusion.262
  434.0 0.8 copy-done.1
  434.8 2.1 fusion.264
  437.5 30.5 %all_gather.60 = bf16[8,1,64,128]{3,2,1,0:T(8,128)(2,1)S(1)} all-gather(bf16[1,1,64,128]{3,2,1,0:T(8,128)(2,1)S(1)} %fusion.47), channel_id=1, replica_groups=mesh['group'=2,'fsdp'=2,'tensor'=8] {'tensor'}, dimensions={0}, use_global_device_ids=true | all-gather | bytes 147456 | tf_op jit(solution)/shard_map/all_gather | solution.py:22
  468.1 18.1 %all_gather.59 = bf16[8,1,64]{2,1,0:T(2,128)(2,1)S(1)} all-gather(bf16[1,1,64]{2,1,0:T(2,128)(2,1)S(1)} %convert_element_type.865), channel_id=1, replica_groups=mesh['group'=2,'fsdp'=2,'tensor'=8] {'tensor'}, dimensions={0}, use_global_device_ids=true | all-gather | bytes 1152 | tf_op jit(solution)/shard_map/all_gather | solution.py:22
  486.3 16.2 %all_gather.58 = bf16[8,1,64]{2,1,0:T(2,128)(2,1)S(1)} all-gather(bf16[1,1,64]{2,1,0:T(2,128)(2,1)S(1)} %convert_element_type.861), channel_id=1, replica_groups=mesh['group'=2,'fsdp'=2,'tensor'=8] {'tensor'}, dimensions={0}, use_global_device_ids=true | all-gather | bytes 1152 | tf_op jit(solution)/shard_map/all_gather | solution.py:22
  502.5 1.2 while.78
  503.9 6.0 fusion.266
  510.6 30.5 %all_gather.63 = bf16[8,1,64,128]{3,2,1,0:T(8,128)(2,1)S(1)} all-gather(bf16[1,1,64,128]{3,2,1,0:T(8,128)(2,1)S(1)} %fusion.48), channel_id=1, replica_groups=mesh['group'=2,'fsdp'=2,'tensor'=8] {'tensor'}, dimensions={0}, use_global_device_ids=true | all-gather | bytes 147456 | tf_op jit(solution)/shard_map/all_gather | solution.py:22
  541.2 18.1 %all_gather.62 = bf16[8,1,64]{2,1,0:T(2,128)(2,1)S(1)} all-gather(bf16[1,1,64]{2,1,0:T(2,128)(2,1)S(1)} %convert_element_type.885), channel_id=1, replica_groups=mesh['group'=2,'fsdp'=2,'tensor'=8] {'tensor'}, dimensions={0}, use_global_device_ids=true | all-gather | bytes 1152 | tf_op jit(solution)/shard_map/all_gather | solution.py:22
  559.4 16.2 %all_gather.61 = bf16[8,1,64]{2,1,0:T(2,128)(2,1)S(1)} all-gather(bf16[1,1,64]{2,1,0:T(2,128)(2,1)S(1)} %convert_element_type.881), channel_id=1, replica_groups=mesh['group'=2,'fsdp'=2,'tensor'=8] {'tensor'}, dimensions={0}, use_global_device_ids=true | all-gather | bytes 1152 | tf_op jit(solution)/shard_map/all_gather | solution.py:22
  575.6 1.2 while.79
  577.0 6.1 fusion.268
  583.1 68.1 %all-reduce.8.cloned.1.call-done = (f32[1,5120]{1,0:T(1,128)}, f32[1,5120]{1,0:T(1,128)}, f32[1,5120]{1,0:T(1,128)}, f32[1,5120]{1,0:T(1,128)}) async-done(((f32[1,5120]{1,0:T(1,128)}, f32[1,5120]{1,0:T(1,128)}, f32[1,5120]{1,0:T(1,128)}, f32[1,5120]{1,0:T(1,128)}), (f32[1,5120]{1,0:T(1,128)}, f32[1,5120]{1,0:T(1,128)}, f32[1,5120]{1,0:T(1,128)}, f32[1,5120]{1,0:T(1,128)})) %all-reduce.8.cloned.1.call-update) | async-done | bytes 81936 | tf_op jit(solution)/shard_map/psum | solution.py:234
  651.2 0.9 fusion.91
  652.1 0.7 pad_maximum_fusion
  (242 shorter events, 12.7 us)
Async XLA Ops:
  6.5 412.9 %copy-start = (bf16[1024,128]{1,0:T(8,128)(2,1)S(1)}, bf16[1024,128]{1,0:T(8,128)(2,1)}, u32[]{:S(2)}) copy-start(bf16[1024,128]{1,0:T(8,128)(2,1)} %param.28) | copy-start | bytes 786436
  6.5 10.6 %copy-start.5 = (f32[2,128]{1,0:T(2,128)S(1)}, f32[2,128]{1,0:T(2,128)}, u32[]{:S(2)}) copy-start(f32[2,128]{1,0:T(2,128)} %param.24) | copy-start | bytes 3076
  6.5 95.9 %all-reduce.6.cloned.1.call-start = ((), (), s32[]{:S(2)}) async-start(), calls=%async_computation | async-start | bytes 327680 | tf_op jit(solution)/shard_map/psum | solution.py:132
  11.8 142.6 %all-gather.2.cloned.1.call-start = ((), (), s32[]{:S(2)}) async-start(), calls=%async_computation.1 | async-start | bytes 4177920 | tf_op jit(solution)/shard_map/all_gather | solution.py:93
  12.6 638.6 %all-reduce.8.cloned.1.call-start = ((), (), s32[]{:S(2)}) async-start(), calls=%async_computation.2 | async-start | bytes 163840 | tf_op jit(solution)/shard_map/psum | solution.py:234
  108.1 57.9 %copy-start.3 = (bf16[640,384]{1,0:T(8,128)(2,1)S(1)}, bf16[640,384]{1,0:T(8,128)(2,1)}, u32[]{:S(2)}) copy-start(bf16[640,384]{1,0:T(8,128)(2,1)} %param.27) | copy-start | bytes 1474564
  190.3 8.5 %copy-start.2 = (bf16[640,10240]{1,0:T(8,128)(2,1)S(1)}, bf16[640,10240]{1,0:T(8,128)(2,1)}, u32[]{:S(2)}) copy-start(bf16[640,10240]{1,0:T(8,128)(2,1)} %fusion.41) | copy-start | bytes 39321604
  427.8 7.0 %copy-start.1 = (bf16[1024,5120]{1,0:T(8,128)(2,1)S(1)}, bf16[1024,5120]{1,0:T(8,128)(2,1)}, u32[]{:S(2)}) copy-start(bf16[1024,5120]{1,0:T(8,128)(2,1)} %add_convert_fusion) | copy-start | bytes 31457284
  509.9 141.3 %copy-start.4 = (f32[2,4,5120]{2,1,0:T(4,128)S(1)}, f32[2,4,5120]{2,1,0:T(4,128)}, u32[]{:S(2)}) copy-start(f32[2,4,5120]{2,1,0:T(4,128)} %all-reduce.6.cloned.1.call-done) | copy-start | bytes 491524
Sparse Core Ops, SparseCore 0:
  12.0 90.4 all-reduce.5
  104.7 49.7 all-gather.1
  583.2 67.9 all-reduce.7
where the time goes:
time: 660 us; the launch traced here: 659 us
  blocking collectives  335 us (51%)
  waiting for transfers between devices  200 us (30%)
  matrix products  66.6 us (10%)
  other arithmetic  30.6 us (5%)
  between operations  16.8 us (3%)
  local copies, waits for them, and re-layouts  8.39 us (1%)
    all_gather x12, blocking collectives, combined_all(): lax.all_gather(a.astype(kind), axis)  261 us
    psum x1, waiting for transfers between devices, local(): looked_up = lax.psum(lookup_terms, ('fsdp', 'tensor'))  85.3 us
    psum x1, blocking collectives, local(): projected = lax.psum(partial_qkv, 'tensor').astype(jnp.bfloat16)  74.4 us
    psum x1, waiting for transfers between devices, local(): summed_out = lax.psum(partial_out, 'tensor')  68.1 us
    all_gather x1, waiting for transfers between devices, local(): lax.all_gather(adapter_up_factors, ('fsdp', 'tensor'), axis=1, tiled=True)  46.3 us
    dot_general x4, matrix products, local(): jnp.dot(attended, merged_output_weight, preferred_element_type=jnp.float32)  20.4 us
    convert_element_type x1, other arithmetic, local(): (wqkv.astype(jnp.float32) + ADAPTER_SCALE * weight_delta).astype(jnp.bflo...  18.4 us
  transfers between devices with their start and end apart: 3, of which 3 were waited for; matrix products, arithmetic and copies ran while one was open for 1% of the time, Pallas kernels for 0%

commit v1 on v0

--- a/solution.py
+++ b/solution.py
@@ -3,6 +3,8 @@
 import jax
 import jax.numpy as jnp
 from jax import lax
+from jax.experimental import pallas as pl
+from jax.experimental.pallas import tpu as pltpu
 from jax.sharding import PartitionSpec as P
 
 QUERY_HEADS = 64
@@ -236,6 +238,473 @@
     return jnp.stack(results, axis=1)
 
 
+LANES = 128
+MESH = pl.DeviceIdType.MESH
+
+
+def fused_kernel(
+    n, chunk,
+    rows_ref, length_ref, gain_ref, qk_gain_ref, cos_ref, sin_ref, up_ref,
+    wqkv_hbm, wout_hbm, cache_hbm, down_hbm, down_out_hbm,
+    out_ref,
+    wqkv, wout, cache, down, down_out, up,
+    x_recv, x_rows, part_send, part_recv, proj_send, proj_recv, heads, rotated,
+    soft_send, soft_recv, out_send, out_recv, final_send,
+    load_sem, x_ssem, x_rsem, up_ssem, up_lsem, up_rsem,
+    part_ssem, part_rsem, proj_ssem, proj_rsem, soft_ssem, soft_rsem,
+    out_ssem, out_rsem, final_ssem, final_rsem,
+):
+    f = lax.axis_index("fsdp")
+    t = lax.axis_index("tensor")
+    me = f * n + t
+    in_rows = wqkv.shape[0]
+    blocks = in_rows // LANES
+    width = wqkv.shape[1] // n
+    heads_here = width // LANES
+    slots = cache.shape[0]
+    kv_width = cache.shape[1] // 2
+    model_width = in_rows * n
+    fine = 32
+    q_chunks = width // chunk
+    o_chunks = in_rows // chunk
+    all_q = n * q_chunks
+    f32 = jnp.float32
+
+    loads = [
+        pltpu.make_async_copy(down_hbm, down, load_sem.at[0]),
+        pltpu.make_async_copy(wqkv_hbm, wqkv, load_sem.at[1]),
+        pltpu.make_async_copy(cache_hbm.at[0], cache, load_sem.at[2]),
+        pltpu.make_async_copy(wout_hbm, wout, load_sem.at[3]),
+        pltpu.make_async_copy(down_out_hbm, down_out, load_sem.at[4]),
+    ]
+    for load in loads:
+        load.start()
+
+    barrier = pltpu.get_barrier_semaphore()
+
+    @pl.loop(1, 2 * n)
+    def _(i):
+        peer = lax.rem(me + i, 2 * n)
+        pl.semaphore_signal(
+            barrier, inc=1, device_id={"fsdp": peer // n, "tensor": lax.rem(peer, n)},
+            device_id_type=MESH,
+        )
+
+    pl.semaphore_wait(barrier, 2 * n - 1)
+
+    def x_copy(peer, slot):
+        return pltpu.make_async_remote_copy(
+            src_ref=rows_ref.at[peer], dst_ref=x_recv.at[slot],
+            send_sem=x_ssem.at[peer], recv_sem=x_rsem.at[slot],
+            device_id={"fsdp": peer // n, "tensor": lax.rem(peer, n)}, device_id_type=MESH,
+        )
+
+    @pl.loop(1, 2 * n)
+    def _(i):
+        peer = lax.rem(me + i, 2 * n)
+        x_copy(peer, me).start()
+
+    pieces = up_ref.shape[0]
+
+    def up_route(c):
+        g = pieces * me + c
+        for_q = g < all_q
+        target = jnp.where(for_q, g // q_chunks, (g - all_q) // o_chunks)
+        slot = jnp.where(for_q, lax.rem(g, q_chunks), q_chunks + lax.rem(g, o_chunks))
+        return target, slot
+
+    def up_copy(c, fd):
+        target, slot = up_route(c)
+        return pltpu.make_async_remote_copy(
+            src_ref=up_ref.at[c], dst_ref=up.at[slot],
+            send_sem=up_ssem.at[c, fd], recv_sem=up_rsem.at[slot],
+            device_id={"fsdp": fd, "tensor": target}, device_id_type=MESH,
+        )
+
+    for c in range(pieces):
+        for fd in range(2):
+            target, slot = up_route(c)
+            same = jnp.logical_and(target == t, f == fd)
+
+            @pl.when(same)
+            def _():
+                pltpu.make_async_copy(up_ref.at[c], up.at[slot], up_rsem.at[slot]).start()
+
+            @pl.when(jnp.logical_not(same))
+            def _():
+                up_copy(c, fd).start()
+
+    def peers_copy(src, dst, ssem, rsem, target, slot):
+        return pltpu.make_async_remote_copy(
+            src_ref=src, dst_ref=dst, send_sem=ssem.at[target], recv_sem=rsem.at[slot],
+            device_id={"fsdp": f, "tensor": target}, device_id_type=MESH,
+        )
+
+    x_rows[...] = rows_ref[me].astype(f32)
+
+    @pl.loop(1, 2 * n)
+    def _(i):
+        peer = lax.rem(me + i, 2 * n)
+        x_copy(peer, peer).wait_recv()
+        x_rows[...] += x_recv[peer].astype(f32)
+
+    def flat(values, count):
+        return jnp.concatenate(
+            [values[STEPS * j : STEPS * (j + 1)] for j in range(count)], axis=1
+        )
+
+    def tall(values, count):
+        return jnp.concatenate(
+            [values[:STEPS, LANES * j : LANES * (j + 1)] for j in range(count)], axis=0
+        )
+
+    def nt(a, b):
+        return lax.dot_general(a, b, (((1,), (1,)), ((), ())), preferred_element_type=f32)
+
+    def nt_fine(a, b):
+        high = a.astype(jnp.bfloat16)
+        low = (a - high.astype(f32)).astype(jnp.bfloat16)
+        return nt(high, b) + nt(low, b)
+
+    x = flat(x_rows[...], blocks)
+    gain = gain_ref[:, pl.ds(pl.multiple_of(t * in_rows, LANES), in_rows)].astype(f32)
+    scaled = (x * gain).astype(jnp.bfloat16)
+    square = jnp.broadcast_to(jnp.sum(x * x, axis=1, keepdims=True), (STEPS, LANES))
+    loads[0].wait()
+    low = jnp.dot(scaled, down[...], preferred_element_type=f32)
+    extra = jnp.concatenate([tall(low, 3), square], axis=0)
+    loads[1].wait()
+
+    @pl.loop(0, n)
+    def _(i):
+        target = lax.rem(t + 1 + i, n)
+        part = jnp.dot(
+            scaled, wqkv[:, pl.ds(pl.multiple_of(target * width, LANES), width)],
+            preferred_element_type=f32,
+        )
+        part_send[target] = jnp.concatenate([tall(part, heads_here), extra], axis=0)
+
+        @pl.when(i < n - 1)
+        def _():
+            peers_copy(
+                part_send.at[target], part_recv.at[t], part_ssem, part_rsem, target, t
+            ).start()
+
+    for slot in range(q_chunks):
+        pltpu.make_async_copy(up_ref.at[0], up.at[slot], up_rsem.at[slot]).wait()
+    total = part_send[t]
+    for i in range(1, n):
+        source = lax.rem(t + i, n)
+        peers_copy(
+            part_send.at[source], part_recv.at[source], part_ssem, part_rsem, source, source
+        ).wait_recv()
+        total = total + part_recv[source]
+    base = STEPS * heads_here
+    rate = lax.rsqrt(total[base + 3 * STEPS :] * (1.0 / model_width) + EPSILON)
+    factors = total[base : base + 3 * STEPS]
+    delta = nt_fine(factors, up[:q_chunks].reshape(width, LANES))
+    pieces_out = []
+    for j in range(heads_here):
+        head = t * heads_here + j
+        mine = delta[:, LANES * j : LANES * (j + 1)]
+        picked = jnp.where(
+            head < QUERY_HEADS,
+            mine[:STEPS],
+            jnp.where(head < QUERY_HEADS + KVH, mine[STEPS : 2 * STEPS], mine[2 * STEPS :]),
+        )
+        pieces_out.append((total[STEPS * j : STEPS * (j + 1)] + ADAPTER_SCALE * picked) * rate)
+    spare = proj_send.shape[0] - base
+    pieces_out.append(jnp.zeros((spare, LANES), f32))
+    proj_send[...] = jnp.concatenate(pieces_out, axis=0).astype(jnp.bfloat16)
+
+    @pl.loop(1, n)
+    def _(i):
+        target = lax.rem(t + i, n)
+        peers_copy(proj_send, proj_recv.at[t], proj_ssem, proj_rsem, target, t).start()
+
+    heads[t] = proj_send[...].astype(f32)[:base]
+
+    @pl.loop(1, n)
+    def _(i):
+        source = lax.rem(t + i, n)
+        peers_copy(
+            proj_send, proj_recv.at[source], proj_ssem, proj_rsem, source, source
+        ).wait_recv()
+        heads[source] = proj_recv[source].astype(f32)[:base]
+
+    every = heads[...].reshape(n * base, LANES)
+    q_rows = STEPS * QUERY_HEADS
+    k_rows = STEPS * KVH
+
+    def turned(values, scale):
+        count = values.shape[0]
+        ms = jnp.mean(values * values, axis=1, keepdims=True)
+        values = values * lax.rsqrt(ms + EPSILON) * scale
+        cosine = jnp.concatenate([cos_ref[...]] * (count // 8), axis=0)
+        sine = jnp.concatenate([sin_ref[...]] * (count // 8), axis=0)
+        return (values * cosine + pltpu.roll(values, LANES // 2, 1) * sine).astype(jnp.bfloat16)
+
+    rotated[...] = turned(every[:q_rows], qk_gain_ref[0:1, :])
+    new_keys = turned(every[q_rows : q_rows + k_rows], qk_gain_ref[1:2, :])
+    new_values = every[q_rows + k_rows :].astype(jnp.bfloat16)
+
+    scaling = 1.0 / math.sqrt(HEAD_SIZE)
+    length = length_ref[0]
+    loads[2].wait()
+    place = t * slots + lax.broadcasted_iota(jnp.int32, (1, slots), 1)
+    visible = place < length
+    diagonal = lax.broadcasted_iota(jnp.int32, (fine, LANES), 0) == lax.broadcasted_iota(
+        jnp.int32, (fine, LANES), 1
+    )
+    top_row = lax.broadcasted_iota(jnp.int32, (8, LANES), 0) == 0
+
+    def to_row(column):
+        return jnp.sum(jnp.where(diagonal, column, 0.0), axis=0, keepdims=True)
+
+    def to_column(row):
+        return jnp.sum(jnp.where(diagonal, row, 0.0), axis=1, keepdims=True)
+
+    @pl.loop(0, n)
+    def _(i):
+        g = lax.rem(t + 1 + i, n)
+        query = rotated[pl.ds(pl.multiple_of(g * fine, fine), fine)]
+        keys = cache[:, pl.ds(pl.multiple_of(g * LANES, LANES), LANES)]
+        values = cache[:, pl.ds(pl.multiple_of(kv_width + g * LANES, LANES), LANES)]
+        scores = jnp.where(visible, nt(query, keys) * scaling, -1e30)
+        top = jnp.max(scores, axis=1, keepdims=True)
+        weights = jnp.where(visible, jnp.exp(scores - top), 0.0)
+        count = jnp.sum(weights, axis=1, keepdims=True)
+        soft_send[g, :fine] = jnp.dot(
+            weights.astype(jnp.bfloat16), values, preferred_element_type=f32
+        )
+        soft_send[g, fine:] = jnp.where(top_row, to_row(top), to_row(count))
+
+        @pl.when(i < n - 1)
+        def _():
+            peers_copy(soft_send.at[g], soft_recv.at[t], soft_ssem, soft_rsem, g, t).start()
+
+    own = rotated[pl.ds(pl.multiple_of(t * fine, fine), fine)]
+    fresh = nt(own, new_keys) * scaling
+    row = lax.broadcasted_iota(jnp.int32, (fine, k_rows), 0)
+    col = lax.broadcasted_iota(jnp.int32, (fine, k_rows), 1)
+    allowed = jnp.logical_and(col // STEPS == t, col % STEPS <= row % STEPS)
+    fresh = jnp.where(allowed, fresh, -1e30)
+    fresh_top = jnp.max(fresh, axis=1, keepdims=True)
+
+    soft_recv[t] = soft_send[t]
+    for i in range(1, n):
+        source = lax.rem(t + i, n)
+        peers_copy(
+            soft_send.at[source], soft_recv.at[source], soft_ssem, soft_rsem, source, source
+        ).wait_recv()
+    tops = [to_column(soft_recv[i, fine : fine + 1]) for i in range(n)]
+    largest = fresh_top
+    for top in tops:
+        largest = jnp.maximum(largest, top)
+    weights = jnp.where(allowed, jnp.exp(fresh - largest), 0.0)
+    denominator = jnp.sum(weights, axis=1, keepdims=True)
+    numerator = jnp.dot(weights.astype(jnp.bfloat16), new_values, preferred_element_type=f32)
+    for i in range(n):
+        factor = jnp.exp(tops[i] - largest)
+        denominator += factor * to_column(soft_recv[i, fine + 1 : fine + 2])
+        numerator += factor * soft_recv[i, :fine]
+    attended = flat(numerator / denominator, fine // STEPS).astype(jnp.bfloat16)
+
+    loads[3].wait()
+    loads[4].wait()
+    low_out = jnp.dot(attended, down_out[...], preferred_element_type=f32)
+
+    @pl.loop(0, n)
+    def _(i):
+        target = lax.rem(t + 1 + i, n)
+        part = jnp.dot(
+            attended, wout[:, pl.ds(pl.multiple_of(target * in_rows, LANES), in_rows)],
+            preferred_element_type=f32,
+        )
+        out_send[target] = jnp.concatenate([tall(part, blocks), low_out], axis=0)
+
+        @pl.when(i < n - 1)
+        def _():
+            peers_copy(
+                out_send.at[target], out_recv.at[t], out_ssem, out_rsem, target, t
+            ).start()
+
+    for slot in range(q_chunks, q_chunks + o_chunks):
+        pltpu.make_async_copy(up_ref.at[0], up.at[slot], up_rsem.at[slot]).wait()
+    summed = out_send[t]
+    for i in range(1, n):
+        source = lax.rem(t + i, n)
+        peers_copy(
+            out_send.at[source], out_recv.at[source], out_ssem, out_rsem, source, source
+        ).wait_recv()
+        summed = summed + out_recv[source]
+    base_out = STEPS * blocks
+    delta_out = tall(
+        nt_fine(summed[base_out:], up[q_chunks:].reshape(in_rows, LANES)), blocks
+    )
+    hidden = x_rows[:base_out] + summed[:base_out] + ADAPTER_SCALE * delta_out
+    spare_out = final_send.shape[0] - base_out
+    final_send[...] = jnp.concatenate(
+        [hidden, jnp.zeros((spare_out, LANES), f32)], axis=0
+    ).astype(jnp.bfloat16)
+
+    @pl.loop(1, n)
+    def _(i):
+        target = lax.rem(t + i, n)
+        peers_copy(final_send, out_ref.at[t], final_ssem, final_rsem, target, t).start()
+
+    out_ref[t] = final_send[...]
+
+    @pl.loop(1, n)
+    def _(i):
+        source = lax.rem(t + i, n)
+        peers_copy(
+            final_send, out_ref.at[source], final_ssem, final_rsem, source, source
+        ).wait_recv()
+
+    @pl.loop(1, 2 * n)
+    def _(i):
+        peer = lax.rem(me + i, 2 * n)
+        x_copy(peer, me).wait_send()
+
+    for c in range(pieces):
+        for fd in range(2):
+            target, slot = up_route(c)
+
+            @pl.when(jnp.logical_not(jnp.logical_and(target == t, f == fd)))
+            def _():
+                up_copy(c, fd).wait_send()
+
+    @pl.loop(1, n)
+    def _(i):
+        target = lax.rem(t + i, n)
+        peers_copy(
+            part_send.at[target], part_recv.at[t], part_ssem, part_rsem, target, t
+        ).wait_send()
+        peers_copy(proj_send, proj_recv.at[t], proj_ssem, proj_rsem, target, t).wait_send()
+        peers_copy(
+            soft_send.at[target], soft_recv.at[t], soft_ssem, soft_rsem, target, t
+        ).wait_send()
+        peers_copy(
+            out_send.at[target], out_recv.at[t], out_ssem, out_rsem, target, t
+        ).wait_send()
+        peers_copy(final_send, out_ref.at[t], final_ssem, final_rsem, target, t).wait_send()
+
+
+def up_to(count, multiple):
+    return -(-count // multiple) * multiple
+
+
+def fused(
+    step_token_rows,
+    token_embedding_table,
+    cached_row_lengths,
+    key_value_cache,
+    input_norm_gain,
+    query_key_gains,
+    wqkv,
+    wout,
+    adapter_down_projections,
+    adapter_down_output,
+    adapter_up_factors,
+):
+    n = lax.axis_size("tensor")
+    f = lax.axis_index("fsdp")
+    t = lax.axis_index("tensor")
+    in_rows, projection_width = wqkv.shape
+    model_width = wout.shape[1]
+    width = projection_width // n
+    shard_rows = token_embedding_table.shape[0]
+    shard = adapter_up_factors.shape[1]
+    chunk = math.gcd(math.gcd(shard, width), in_rows)
+    pieces = shard // chunk
+    blocks = in_rows // LANES
+    heads_here = width // LANES
+    bf16, f32 = jnp.bfloat16, jnp.float32
+
+    local_ids = step_token_rows.reshape(-1) - (f * n + t) * shard_rows
+    held = jnp.logical_and(local_ids >= 0, local_ids < shard_rows)
+    rows = jnp.where(
+        held[:, None], token_embedding_table[jnp.clip(local_ids, 0, shard_rows - 1)], 0
+    ).astype(bf16)
+    rows = rows.reshape(2, STEPS, n, blocks, LANES).transpose(0, 2, 3, 1, 4)
+    rows = rows.reshape(2 * n, STEPS * blocks, LANES)
+    x_tall = up_to(STEPS * blocks, 16)
+    rows = jnp.pad(rows, ((0, 0), (0, x_tall - STEPS * blocks), (0, 0)))
+
+    half = HEAD_SIZE // 2
+    inverse = ROPE_BASE ** (-(2.0 * jnp.arange(half, dtype=f32)) / HEAD_SIZE)
+    position = (cached_row_lengths[0] + jnp.arange(8, dtype=jnp.int32) % STEPS).astype(f32)
+    angle = position[:, None] * inverse
+    cosine = jnp.cos(angle)
+    sine = jnp.sin(angle)
+    cosine = jnp.concatenate([cosine, cosine], axis=1)
+    sine = jnp.concatenate([-sine, sine], axis=1)
+    up = adapter_up_factors.T.reshape(pieces, chunk, LANES)
+
+    part_rows = STEPS * (heads_here + 4)
+    proj_rows = up_to(STEPS * heads_here, 16)
+    soft_rows = 32 + 8
+    out_rows = STEPS * (blocks + 1)
+    slots_up = (width + in_rows) // chunk
+    vmem = pl.BlockSpec(memory_space=pltpu.VMEM)
+    smem = pl.BlockSpec(memory_space=pltpu.SMEM)
+    hbm = pl.BlockSpec(memory_space=pl.ANY)
+    dma = pltpu.SemaphoreType.DMA
+    result = pl.pallas_call(
+        lambda *refs: fused_kernel(n, chunk, *refs),
+        out_shape=jax.ShapeDtypeStruct((n, x_tall, LANES), bf16),
+        in_specs=[vmem, smem, vmem, vmem, vmem, vmem, vmem] + [hbm] * 5,
+        out_specs=vmem,
+        scratch_shapes=[
+            pltpu.VMEM(wqkv.shape, bf16),
+            pltpu.VMEM(wout.shape, bf16),
+            pltpu.VMEM(key_value_cache.shape[1:], bf16),
+            pltpu.VMEM(adapter_down_projections.shape, bf16),
+            pltpu.VMEM(adapter_down_output.shape, bf16),
+            pltpu.VMEM((slots_up, chunk, LANES), bf16),
+            pltpu.VMEM((2 * n, x_tall, LANES), bf16),
+            pltpu.VMEM((x_tall, LANES), f32),
+            pltpu.VMEM((n, part_rows, LANES), f32),
+            pltpu.VMEM((n, part_rows, LANES), f32),
+            pltpu.VMEM((proj_rows, LANES), bf16),
+            pltpu.VMEM((n, proj_rows, LANES), bf16),
+            pltpu.VMEM((n, STEPS * heads_here, LANES), f32),
+            pltpu.VMEM((STEPS * QUERY_HEADS, LANES), bf16),
+            pltpu.VMEM((n, soft_rows, LANES), f32),
+            pltpu.VMEM((n, soft_rows, LANES), f32),
+            pltpu.VMEM((n, out_rows, LANES), f32),
+            pltpu.VMEM((n, out_rows, LANES), f32),
+            pltpu.VMEM((x_tall, LANES), bf16),
+            dma((5,)),
+            dma((2 * n,)),
+            dma((2 * n,)),
+            dma((pieces, 2)),
+            dma((slots_up,)),
+            dma((slots_up,)),
+        ]
+        + [dma((n,))] * 10,
+        compiler_params=pltpu.CompilerParams(
+            collective_id=0, has_side_effects=True, vmem_limit_bytes=52 * 1024 * 1024
+        ),
+    )(
+        rows,
+        cached_row_lengths,
+        input_norm_gain.reshape(1, model_width),
+        query_key_gains,
+        cosine,
+        sine,
+        up,
+        wqkv,
+        wout,
+        key_value_cache,
+        adapter_down_projections,
+        adapter_down_output,
+    )
+    result = result[:, : STEPS * blocks].reshape(n, blocks, STEPS, LANES)
+    return result.transpose(2, 0, 1, 3).reshape(1, STEPS, model_width)
+
+
 def solution(mesh):
     in_specs = (
         P("group", None),
@@ -251,4 +720,11 @@
         P(None, ("fsdp", "tensor")),
     )
     out_specs = P(("group", "fsdp"), None, None)
-    return jax.shard_map(local, mesh=mesh, in_specs=in_specs, out_specs=out_specs, check_vma=False)
+    fits = (
+        mesh.shape["tensor"] == KVH
+        and mesh.shape["fsdp"] == 2
+        and HEAD_SIZE == LANES
+        and ADAPTER_RANK == LANES
+    )
+    body = fused if fits else local
+    return jax.shard_map(body, mesh=mesh, in_specs=in_specs, out_specs=out_specs, check_vma=False)

time: 660 us -> 60.5 us (0.09)
  blocking collectives: 335 us -> 0 us
  waiting for transfers between devices: 200 us -> 0 us
  matrix products: 66.6 us -> 0 us
  Pallas kernels: 0 us -> 48.3 us
  other arithmetic: 30.6 us -> 1.67 us
  between operations: 16.8 us -> 0.74 us
    all_gather x12 -> x0, blocking collectives: 261 us -> none  [combined_all(): lax.all_gather(a.astype(kind), axis)]
    psum x2 -> x0, waiting for transfers between devices: 153 us -> none  [the longest x1 85.3 us: local(): looked_up = lax.psum(lookup_terms, ('fsdp', 'tensor'))]
    psum x1 -> x0, blocking collectives: 74.4 us -> none  [local(): projected = lax.psum(partial_qkv, 'tensor').astype(jnp.bfloat16)]
    dot_general x28 -> x0, matrix products: 66.6 us -> none  [the longest x4 20.4 us: local(): jnp.dot(attended, merged_output_weight, preferred_element_type=jnp.float32)]
    pallas_call x0 -> x1, Pallas kernels: none -> 48.3 us  [fused(): pl.pallas_call(lambda *refs: fused_kernel(n, chunk, *refs), out_shape=jax...]
    all_gather x1 -> x0, waiting for transfers between devices: 46.3 us -> none  [local(): lax.all_gather(adapter_up_factors, ('fsdp', 'tensor'), axis=1, tiled=True)]
    convert_element_type x23 -> x1, other arithmetic: 19.5 us -> 0.01 us  [fused(): (cached_row_lengths[0] + jnp.arange(8, dtype=jnp.int32) % STEPS).astype(f32)]
  transfers between devices with their start and end apart: 3 -> 0, of which waited for: 3 -> 0; matrix products, arithmetic and copies ran while one was open for 1% -> 0% of each run, Pallas kernels for 0% -> 0%
where the time goes in v1:
time: 60.5 us; the launch traced here: 60.2 us
  Pallas kernels  48.3 us (80%)
  local copies, waits for them, and re-layouts  9.48 us (16%)
  other arithmetic  1.67 us (3%)
  between operations  0.74 us (1%)
    pallas_call x1, Pallas kernels, fused(): pl.pallas_call(lambda *refs: fused_kernel(n, chunk, *refs), out_shape=jax...  48.3 us
    gather x2, local copies, waits for them, and re-layouts, fused(): token_embedding_table[jnp.clip(local_ids, 0, shard_rows - 1)]  4.33 us
    unnamed x8, local copies, waits for them, and re-layouts  3.61 us

profile of v1, /device:TPU:0, one launch (start us, length us, event | category | flops | bytes accessed | tf_op | source)
XLA Modules:
  0.0 60.2 jit_solution(245289414519911519)
XLA Ops:
  0.0 0.7 %subtract_clamp_fusion = s32[2,4]{1,0:T(2,128)S(1)} fusion(s32[2,4]{1,0:T(2,128)} %param.11, s32[]{:T(128)S(6)} %mul.30), kind=kLoop, calls=%fused_computation.11 | loop fusion | flops 16 | bytes 68 | tf_op jit(solution)/shard_map/jit(clip)/min | solution.py:628
  0.7 0.1 min.12
  0.8 4.2 %gather_fusion = bf16[8,5120]{1,0:T(8,128)(2,1)S(1)} fusion(bf16[600,5120]{1,0:T(8,128)(2,1)} %param.12, s32[1024]{0:T(1024)S(1)} %pad_clamp_fusion), kind=kCustom, calls=%fused_computation | custom fusion | bytes 163872 | tf_op jit(solution)/shard_map/gather | solution.py:628
  5.0 0.1 gather.6
  5.1 0.7 %compare_and_fusion = pred[2,4]{1,0:T(4,128)(4,1)S(1)} fusion(s32[2,4]{1,0:T(2,128)} %param.11, s32[]{:T(128)S(6)} %mul.30), kind=kLoop, calls=%fused_computation.9 | loop fusion | flops 32 | bytes 44 | tf_op jit(solution)/shard_map/and | solution.py:626
  5.8 0.1 select_bitcast_fusion
  6.6 0.7 %reshape.74.refs_2_ = bf16[1,5120]{1,0:T(2,128)(2,1)S(1)} reshape(bf16[5120]{0:T(1024)(128)(2,1)} %param.15) | data formatting | bytes 20480 | tf_op jit(solution)/shard_map/reshape | solution.py:693
  7.4 0.1 fusion
  7.5 0.1 pad_maximum_fusion
  7.6 0.0 copy-start
  7.6 1.0 %copy-done = bf16[640,384]{1,0:T(8,128)(2,1)S(1)} copy-done((bf16[640,384]{1,0:T(8,128)(2,1)S(1)}, bf16[640,384]{1,0:T(8,128)(2,1)}, u32[]{:S(2)}) %copy-start) | copy-done | bytes 491544
  8.6 0.0 copy-start.1
  8.6 0.9 %copy-done.1 = bf16[1024,128]{1,0:T(8,128)(2,1)S(1)} copy-done((bf16[1024,128]{1,0:T(8,128)(2,1)S(1)}, bf16[1024,128]{1,0:T(8,128)(2,1)}, u32[]{:S(2)}) %copy-start.1) | copy-done | bytes 262168
  9.6 0.0 copy-start.2
  9.6 0.9 %copy-done.2 = bf16[128,960]{0,1:T(8,128)(2,1)S(1)} copy-done((bf16[128,960]{0,1:T(8,128)(2,1)S(1)}, bf16[128,960]{0,1:T(8,128)(2,1)}, u32[]{:S(2)}) %copy-start.2) | copy-done | bytes 245784
  10.5 0.0 copy-start.3
  10.5 0.7 %copy-done.3 = f32[2,128]{1,0:T(2,128)S(1)} copy-done((f32[2,128]{1,0:T(2,128)S(1)}, f32[2,128]{1,0:T(2,128)}, u32[]{:S(2)}) %copy-start.3) | copy-done | bytes 1048
  11.2 48.3 %shard_map.109 = bf16[8,32,128]{2,1,0:T(8,128)(2,1)S(1)} custom-call(bf16[16,32,128]{2,1,0:T(8,128)(2,1)S(1)} %pad.4.refs_0_, s32[1]{0:T(128)} %copy.18.refs_1_, bf16[1,5120]{1,0:T(2,128)(2,1)S(1)} %reshape.74.refs_2_, f32[2,128]{1,0:T(2,128)S(1)} %copy-done.3, f32[8,128]{1,0:T(8,128)S(1)} %get-tuple-element.8.refs_4_, ...), custom_call_target="tpu_custom_call" | custom-call | tf_op jit(solution)/shard_map/pallas_call | solution.py:654
  59.5 0.7 %reshape.77 = bf16[1,4,5120]{2,1,0:T(4,128)(2,1)} reshape(bf16[4,8,5,128]{3,2,1,0:T(8,128)(2,1)S(1)} %copy.17) | data formatting | bytes 81920 | tf_op jit(solution)/shard_map/reshape | solution.py:705
  (10 shorter events, 0.1 us)
Async XLA Ops:
  7.6 1.0 %copy-start = (bf16[640,384]{1,0:T(8,128)(2,1)S(1)}, bf16[640,384]{1,0:T(8,128)(2,1)}, u32[]{:S(2)}) copy-start(bf16[640,384]{1,0:T(8,128)(2,1)} %refs_10_.1) | copy-start | bytes 1474564
  8.6 0.9 %copy-start.1 = (bf16[1024,128]{1,0:T(8,128)(2,1)S(1)}, bf16[1024,128]{1,0:T(8,128)(2,1)}, u32[]{:S(2)}) copy-start(bf16[1024,128]{1,0:T(8,128)(2,1)} %refs_11_.1) | copy-start | bytes 786436
  9.6 0.9 %copy-start.2 = (bf16[128,960]{0,1:T(8,128)(2,1)S(1)}, bf16[128,960]{0,1:T(8,128)(2,1)}, u32[]{:S(2)}) copy-start(bf16[128,960]{0,1:T(8,128)(2,1)} %param.21) | copy-start | bytes 737284
  10.5 0.7 %copy-start.3 = (f32[2,128]{1,0:T(2,128)S(1)}, f32[2,128]{1,0:T(2,128)}, u32[]{:S(2)}) copy-start(f32[2,128]{1,0:T(2,128)} %refs_3_.1) | copy-start | bytes 3076

commit v2 on v1

--- a/solution.py
+++ b/solution.py
@@ -244,10 +244,10 @@
 
 def fused_kernel(
     n, chunk,
-    rows_ref, length_ref, gain_ref, qk_gain_ref, cos_ref, sin_ref, up_ref,
+    ids_ref, length_ref, gain_ref, cos_ref, sin_ref, qk_gain_hbm, up_ref, table_hbm,
     wqkv_hbm, wout_hbm, cache_hbm, down_hbm, down_out_hbm,
     out_ref,
-    wqkv, wout, cache, down, down_out, up,
+    table, wqkv, wout, cache, down, down_out, qk_gain_ref, up, x_send,
     x_recv, x_rows, part_send, part_recv, proj_send, proj_recv, heads, rotated,
     soft_send, soft_recv, out_send, out_recv, final_send,
     load_sem, x_ssem, x_rsem, up_ssem, up_lsem, up_rsem,
@@ -271,6 +271,8 @@
     f32 = jnp.float32
 
     loads = [
+        pltpu.make_async_copy(table_hbm, table, load_sem.at[5]),
+        pltpu.make_async_copy(qk_gain_hbm, qk_gain_ref, load_sem.at[6]),
         pltpu.make_async_copy(down_hbm, down, load_sem.at[0]),
         pltpu.make_async_copy(wqkv_hbm, wqkv, load_sem.at[1]),
         pltpu.make_async_copy(cache_hbm.at[0], cache, load_sem.at[2]),
@@ -294,15 +296,43 @@
 
     def x_copy(peer, slot):
         return pltpu.make_async_remote_copy(
-            src_ref=rows_ref.at[peer], dst_ref=x_recv.at[slot],
+            src_ref=x_send.at[peer], dst_ref=x_recv.at[slot],
             send_sem=x_ssem.at[peer], recv_sem=x_rsem.at[slot],
             device_id={"fsdp": peer // n, "tensor": lax.rem(peer, n)}, device_id_type=MESH,
         )
 
-    @pl.loop(1, 2 * n)
-    def _(i):
-        peer = lax.rem(me + i, 2 * n)
-        x_copy(peer, me).start()
+    shard_rows = table.shape[0]
+    tokens = lax.broadcasted_iota(jnp.int32, (2 * STEPS, shard_rows), 0)
+    local_row = lax.broadcasted_iota(jnp.int32, (2 * STEPS, shard_rows), 1) + me * shard_rows
+    wanted = jnp.zeros((2 * STEPS, shard_rows), jnp.int32)
+    for k in range(2 * STEPS):
+        wanted = jnp.where(tokens == k, ids_ref[k // STEPS, k % STEPS], wanted)
+    one_hot = jnp.where(wanted == local_row, 1.0, 0.0).astype(jnp.bfloat16)
+    x_pad = jnp.zeros((x_rows.shape[0] - STEPS * blocks, LANES), f32)
+    loads[0].wait()
+
+    @pl.loop(0, n)
+    def _(i):
+        target = lax.rem(t + 1 + i, n)
+        found = jnp.dot(
+            one_hot, table[:, pl.ds(pl.multiple_of(target * in_rows, LANES), in_rows)],
+            preferred_element_type=f32,
+        )
+        for fd in range(2):
+            mine = jnp.concatenate(
+                [
+                    found[STEPS * fd : STEPS * (fd + 1), LANES * j : LANES * (j + 1)]
+                    for j in range(blocks)
+                ]
+                + [x_pad],
+                axis=0,
+            )
+            peer = fd * n + target
+            x_send[peer] = mine.astype(jnp.bfloat16)
+
+            @pl.when(peer != me)
+            def _():
+                x_copy(peer, me).start()
 
     pieces = up_ref.shape[0]
 
@@ -340,7 +370,7 @@
             device_id={"fsdp": f, "tensor": target}, device_id_type=MESH,
         )
 
-    x_rows[...] = rows_ref[me].astype(f32)
+    x_rows[...] = x_send[me].astype(f32)
 
     @pl.loop(1, 2 * n)
     def _(i):
@@ -370,10 +400,10 @@
     gain = gain_ref[:, pl.ds(pl.multiple_of(t * in_rows, LANES), in_rows)].astype(f32)
     scaled = (x * gain).astype(jnp.bfloat16)
     square = jnp.broadcast_to(jnp.sum(x * x, axis=1, keepdims=True), (STEPS, LANES))
-    loads[0].wait()
+    loads[2].wait()
     low = jnp.dot(scaled, down[...], preferred_element_type=f32)
     extra = jnp.concatenate([tall(low, 3), square], axis=0)
-    loads[1].wait()
+    loads[3].wait()
 
     @pl.loop(0, n)
     def _(i):
@@ -444,13 +474,14 @@
         sine = jnp.concatenate([sin_ref[...]] * (count // 8), axis=0)
         return (values * cosine + pltpu.roll(values, LANES // 2, 1) * sine).astype(jnp.bfloat16)
 
+    loads[1].wait()
     rotated[...] = turned(every[:q_rows], qk_gain_ref[0:1, :])
     new_keys = turned(every[q_rows : q_rows + k_rows], qk_gain_ref[1:2, :])
     new_values = every[q_rows + k_rows :].astype(jnp.bfloat16)
 
     scaling = 1.0 / math.sqrt(HEAD_SIZE)
     length = length_ref[0]
-    loads[2].wait()
+    loads[4].wait()
     place = t * slots + lax.broadcasted_iota(jnp.int32, (1, slots), 1)
     visible = place < length
     diagonal = lax.broadcasted_iota(jnp.int32, (fine, LANES), 0) == lax.broadcasted_iota(
@@ -510,8 +541,8 @@
         numerator += factor * soft_recv[i, :fine]
     attended = flat(numerator / denominator, fine // STEPS).astype(jnp.bfloat16)
 
-    loads[3].wait()
-    loads[4].wait()
+    loads[5].wait()
+    loads[6].wait()
     low_out = jnp.dot(attended, down_out[...], preferred_element_type=f32)
 
     @pl.loop(0, n)
@@ -609,12 +640,9 @@
     adapter_up_factors,
 ):
     n = lax.axis_size("tensor")
-    f = lax.axis_index("fsdp")
-    t = lax.axis_index("tensor")
     in_rows, projection_width = wqkv.shape
     model_width = wout.shape[1]
     width = projection_width // n
-    shard_rows = token_embedding_table.shape[0]
     shard = adapter_up_factors.shape[1]
     chunk = math.gcd(math.gcd(shard, width), in_rows)
     pieces = shard // chunk
@@ -622,15 +650,7 @@
     heads_here = width // LANES
     bf16, f32 = jnp.bfloat16, jnp.float32
 
-    local_ids = step_token_rows.reshape(-1) - (f * n + t) * shard_rows
-    held = jnp.logical_and(local_ids >= 0, local_ids < shard_rows)
-    rows = jnp.where(
-        held[:, None], token_embedding_table[jnp.clip(local_ids, 0, shard_rows - 1)], 0
-    ).astype(bf16)
-    rows = rows.reshape(2, STEPS, n, blocks, LANES).transpose(0, 2, 3, 1, 4)
-    rows = rows.reshape(2 * n, STEPS * blocks, LANES)
     x_tall = up_to(STEPS * blocks, 16)
-    rows = jnp.pad(rows, ((0, 0), (0, x_tall - STEPS * blocks), (0, 0)))
 
     half = HEAD_SIZE // 2
     inverse = ROPE_BASE ** (-(2.0 * jnp.arange(half, dtype=f32)) / HEAD_SIZE)
@@ -654,15 +674,18 @@
     result = pl.pallas_call(
         lambda *refs: fused_kernel(n, chunk, *refs),
         out_shape=jax.ShapeDtypeStruct((n, x_tall, LANES), bf16),
-        in_specs=[vmem, smem, vmem, vmem, vmem, vmem, vmem] + [hbm] * 5,
+        in_specs=[smem, smem, vmem, vmem, vmem] + [hbm] * 8,
         out_specs=vmem,
         scratch_shapes=[
+            pltpu.VMEM(token_embedding_table.shape, bf16),
             pltpu.VMEM(wqkv.shape, bf16),
             pltpu.VMEM(wout.shape, bf16),
             pltpu.VMEM(key_value_cache.shape[1:], bf16),
             pltpu.VMEM(adapter_down_projections.shape, bf16),
             pltpu.VMEM(adapter_down_output.shape, bf16),
+            pltpu.VMEM(query_key_gains.shape, f32),
             pltpu.VMEM((slots_up, chunk, LANES), bf16),
+            pltpu.VMEM((2 * n, x_tall, LANES), bf16),
             pltpu.VMEM((2 * n, x_tall, LANES), bf16),
             pltpu.VMEM((x_tall, LANES), f32),
             pltpu.VMEM((n, part_rows, LANES), f32),
@@ -676,7 +699,7 @@
             pltpu.VMEM((n, out_rows, LANES), f32),
             pltpu.VMEM((n, out_rows, LANES), f32),
             pltpu.VMEM((x_tall, LANES), bf16),
-            dma((5,)),
+            dma((7,)),
             dma((2 * n,)),
             dma((2 * n,)),
             dma((pieces, 2)),
@@ -685,16 +708,17 @@
         ]
         + [dma((n,))] * 10,
         compiler_params=pltpu.CompilerParams(
-            collective_id=0, has_side_effects=True, vmem_limit_bytes=52 * 1024 * 1024
+            collective_id=0, has_side_effects=True, vmem_limit_bytes=60 * 1024 * 1024
         ),
     )(
-        rows,
+        step_token_rows,
         cached_row_lengths,
         input_norm_gain.reshape(1, model_width),
-        query_key_gains,
         cosine,
         sine,
+        query_key_gains,
         up,
+        token_embedding_table,
         wqkv,
         wout,
         key_value_cache,

time: 60.5 us -> 55.9 us (0.924)
  local copies, waits for them, and re-layouts: 9.48 us -> 2.81 us
  Pallas kernels: 48.3 us -> 51.3 us
  other arithmetic: 1.67 us -> 0.81 us
    gather x2 -> x0, local copies, waits for them, and re-layouts: 4.33 us -> none  [fused(): token_embedding_table[jnp.clip(local_ids, 0, shard_rows - 1)]]
    unnamed x8 -> x0, local copies, waits for them, and re-layouts: 3.61 us -> none
    pallas_call x1, Pallas kernels: 48.3 us -> 51.3 us  [fused(): pl.pallas_call(lambda *refs: fused_kernel(n, chunk, *refs), out_shape=jax...]
    slice x2, local copies, waits for them, and re-layouts: 0.02 us -> 0.82 us  [fused(): result = result[:, :STEPS * blocks].reshape(n, blocks, STEPS, LANES)]
    and x1 -> x0, other arithmetic: 0.69 us -> none  [fused(): held = jnp.logical_and(local_ids >= 0, local_ids < shard_rows)]
    min x1 -> x0, other arithmetic: 0.68 us -> none  [fused(): jnp.clip(local_ids, 0, shard_rows - 1)]
where the time goes in v2:
time: 55.9 us; the launch traced here: 55.6 us
  Pallas kernels  51.3 us (92%)
  local copies, waits for them, and re-layouts  2.81 us (5%)
  other arithmetic  0.81 us (1%)
  between operations  0.68 us (1%)
    pallas_call x1, Pallas kernels, fused(): pl.pallas_call(lambda *refs: fused_kernel(n, chunk, *refs), out_shape=jax...  51.3 us
    reshape x1, local copies, waits for them, and re-layouts, fused(): input_norm_gain.reshape(1, model_width)  1.32 us

profile of v2, /device:TPU:0, one launch (start us, length us, event | category | flops | bytes accessed | tf_op | source)
XLA Modules:
  0.0 55.6 jit_solution(2411496473693143565)
XLA Ops:
  0.7 0.1 fusion
  0.8 0.7 %pad_maximum_fusion = (f32[8,128]{1,0:T(8,128)}, f32[8,128]{1,0:T(8,128)}) fusion(f32[8,64]{1,0:T(8,128)S(1)} %get-tuple-element.7, f32[8,64]{1,0:T(8,128)S(1)} %get-tuple-element.6, f32[8,64]{1,0:T(8,128)S(1)} %get-tuple-element.5), kind=kLoop, calls=%fused_computation.2 | loop fusion | flops 2048 | bytes 14336 | tf_op jit(solution)/shard_map/concatenate | solution.py:661
  1.5 1.3 %reshape.30.refs_2_ = bf16[1,5120]{1,0:T(2,128)(2,1)} reshape(bf16[5120]{0:T(1024)(128)(2,1)} %param.15) | data formatting | bytes 20480 | tf_op jit(solution)/shard_map/reshape | solution.py:716
  2.8 51.3 %shard_map.109 = bf16[8,32,128]{2,1,0:T(8,128)(2,1)} custom-call(s32[2,4]{1,0:T(2,128)} %refs_0_.1, s32[1]{0:T(128)} %copy.15.refs_1_, bf16[1,5120]{1,0:T(2,128)(2,1)} %reshape.30.refs_2_, f32[8,128]{1,0:T(8,128)} %get-tuple-element.8.refs_3_, f32[8,128]{1,0:T(8,128)} %get-tuple-element.9.refs_4_, f32[2,128]{1,0:T(2,128)} %refs_5_.1, ...), custom_call_target="tpu_custom_call" | custom-call | tf_op jit(solution)/shard_map/pallas_call | solution.py:674
  54.1 0.8 %slice.3 = bf16[8,20,128]{2,1,0:T(8,128)(2,1)S(1)} slice(bf16[8,32,128]{2,1,0:T(8,128)(2,1)} %shard_map.109), slice={[0:8], [0:20], [0:128]} | slice | bytes 81920 | tf_op jit(solution)/shard_map/slice | solution.py:728
  54.9 0.7 %reshape.33 = bf16[1,4,5120]{2,1,0:T(4,128)(2,1)} reshape(bf16[4,8,5,128]{3,2,1,0:T(8,128)(2,1)S(1)} %copy.14) | data formatting | bytes 81920 | tf_op jit(solution)/shard_map/reshape | solution.py:729
  (4 shorter events, 0.1 us)

commit v3 on v2

--- a/solution.py
+++ b/solution.py
@@ -292,8 +292,6 @@
             device_id_type=MESH,
         )
 
-    pl.semaphore_wait(barrier, 2 * n - 1)
-
     def x_copy(peer, slot):
         return pltpu.make_async_remote_copy(
             src_ref=x_send.at[peer], dst_ref=x_recv.at[slot],
@@ -327,12 +325,13 @@
                 + [x_pad],
                 axis=0,
             )
-            peer = fd * n + target
-            x_send[peer] = mine.astype(jnp.bfloat16)
-
-            @pl.when(peer != me)
-            def _():
-                x_copy(peer, me).start()
+            x_send[fd * n + target] = mine.astype(jnp.bfloat16)
+
+    pl.semaphore_wait(barrier, 2 * n - 1)
+
+    @pl.loop(1, 2 * n)
+    def _(i):
+        x_copy(lax.rem(me + i, 2 * n), me).start()
 
     pieces = up_ref.shape[0]
 
@@ -343,26 +342,60 @@
         slot = jnp.where(for_q, lax.rem(g, q_chunks), q_chunks + lax.rem(g, o_chunks))
         return target, slot
 
-    def up_copy(c, fd):
+    def up_copy(c):
         target, slot = up_route(c)
         return pltpu.make_async_remote_copy(
             src_ref=up_ref.at[c], dst_ref=up.at[slot],
-            send_sem=up_ssem.at[c, fd], recv_sem=up_rsem.at[slot],
-            device_id={"fsdp": fd, "tensor": target}, device_id_type=MESH,
-        )
-
-    for c in range(pieces):
-        for fd in range(2):
+            send_sem=up_ssem.at[c], recv_sem=up_rsem.at[slot],
+            device_id={"fsdp": f, "tensor": target}, device_id_type=MESH,
+        )
+
+    def up_spread(for_q):
+        for c in range(pieces):
             target, slot = up_route(c)
-            same = jnp.logical_and(target == t, f == fd)
-
-            @pl.when(same)
+            chosen = (pieces * me + c < all_q) == for_q
+
+            @pl.when(jnp.logical_and(chosen, target == t))
             def _():
                 pltpu.make_async_copy(up_ref.at[c], up.at[slot], up_rsem.at[slot]).start()
 
-            @pl.when(jnp.logical_not(same))
+            @pl.when(jnp.logical_and(chosen, target != t))
             def _():
-                up_copy(c, fd).start()
+                up_copy(c).start()
+
+    def up_pass(slot):
+        return pltpu.make_async_remote_copy(
+            src_ref=up.at[slot], dst_ref=up.at[slot],
+            send_sem=up_lsem.at[slot], recv_sem=up_rsem.at[slot],
+            device_id={"fsdp": 1 - f, "tensor": t}, device_id_type=MESH,
+        )
+
+    def up_from_here(slot):
+        if slot < q_chunks:
+            g = t * q_chunks + slot
+        else:
+            g = all_q + t * o_chunks + slot - q_chunks
+        return g // (pieces * n) == f
+
+    def up_wait(slot):
+        pltpu.make_async_copy(up_ref.at[0], up.at[slot], up_rsem.at[slot]).wait()
+
+    def up_forward(span):
+        for slot in span:
+            @pl.when(up_from_here(slot))
+            def _():
+                up_wait(slot)
+                up_pass(slot).start()
+
+    def up_finish(span):
+        for slot in span:
+            @pl.when(jnp.logical_not(up_from_here(slot)))
+            def _():
+                up_wait(slot)
+
+    q_span = range(q_chunks)
+    o_span = range(q_chunks, q_chunks + o_chunks)
+    up_spread(True)
 
     def peers_copy(src, dst, ssem, rsem, target, slot):
         return pltpu.make_async_remote_copy(
@@ -402,7 +435,8 @@
     square = jnp.broadcast_to(jnp.sum(x * x, axis=1, keepdims=True), (STEPS, LANES))
     loads[2].wait()
     low = jnp.dot(scaled, down[...], preferred_element_type=f32)
-    extra = jnp.concatenate([tall(low, 3), square], axis=0)
+    part_pad = jnp.zeros((part_send.shape[1] - STEPS * (heads_here + 4), LANES), f32)
+    extra = jnp.concatenate([tall(low, 3), square, part_pad], axis=0)
     loads[3].wait()
 
     @pl.loop(0, n)
@@ -412,7 +446,9 @@
             scaled, wqkv[:, pl.ds(pl.multiple_of(target * width, LANES), width)],
             preferred_element_type=f32,
         )
-        part_send[target] = jnp.concatenate([tall(part, heads_here), extra], axis=0)
+        part_send[target] = jnp.concatenate([tall(part, heads_here), extra], axis=0).astype(
+            jnp.bfloat16
+        )
 
         @pl.when(i < n - 1)
         def _():
@@ -420,17 +456,17 @@
                 part_send.at[target], part_recv.at[t], part_ssem, part_rsem, target, t
             ).start()
 
-    for slot in range(q_chunks):
-        pltpu.make_async_copy(up_ref.at[0], up.at[slot], up_rsem.at[slot]).wait()
-    total = part_send[t]
+    up_forward(q_span)
+    total = part_send[t].astype(f32)
     for i in range(1, n):
         source = lax.rem(t + i, n)
         peers_copy(
             part_send.at[source], part_recv.at[source], part_ssem, part_rsem, source, source
         ).wait_recv()
-        total = total + part_recv[source]
+        total = total + part_recv[source].astype(f32)
     base = STEPS * heads_here
-    rate = lax.rsqrt(total[base + 3 * STEPS :] * (1.0 / model_width) + EPSILON)
+    rate = lax.rsqrt(total[base + 3 * STEPS : base + 4 * STEPS] * (1.0 / model_width) + EPSILON)
+    up_finish(q_span)
     factors = total[base : base + 3 * STEPS]
     delta = nt_fine(factors, up[:q_chunks].reshape(width, LANES))
     pieces_out = []
@@ -452,6 +488,7 @@
         target = lax.rem(t + i, n)
         peers_copy(proj_send, proj_recv.at[t], proj_ssem, proj_rsem, target, t).start()
 
+    up_spread(False)
     heads[t] = proj_send[...].astype(f32)[:base]
 
     @pl.loop(1, n)
@@ -514,6 +551,7 @@
         def _():
             peers_copy(soft_send.at[g], soft_recv.at[t], soft_ssem, soft_rsem, g, t).start()
 
+    up_forward(o_span)
     own = rotated[pl.ds(pl.multiple_of(t * fine, fine), fine)]
     fresh = nt(own, new_keys) * scaling
     row = lax.broadcasted_iota(jnp.int32, (fine, k_rows), 0)
@@ -560,8 +598,6 @@
                 out_send.at[target], out_recv.at[t], out_ssem, out_rsem, target, t
             ).start()
 
-    for slot in range(q_chunks, q_chunks + o_chunks):
-        pltpu.make_async_copy(up_ref.at[0], up.at[slot], up_rsem.at[slot]).wait()
     summed = out_send[t]
     for i in range(1, n):
         source = lax.rem(t + i, n)
@@ -569,6 +605,7 @@
             out_send.at[source], out_recv.at[source], out_ssem, out_rsem, source, source
         ).wait_recv()
         summed = summed + out_recv[source]
+    up_finish(o_span)
     base_out = STEPS * blocks
     delta_out = tall(
         nt_fine(summed[base_out:], up[q_chunks:].reshape(in_rows, LANES)), blocks
@@ -599,12 +636,14 @@
         x_copy(peer, me).wait_send()
 
     for c in range(pieces):
-        for fd in range(2):
-            target, slot = up_route(c)
-
-            @pl.when(jnp.logical_not(jnp.logical_and(target == t, f == fd)))
-            def _():
-                up_copy(c, fd).wait_send()
+        @pl.when(up_route(c)[0] != t)
+        def _():
+            up_copy(c).wait_send()
+
+    for slot in range(q_chunks + o_chunks):
+        @pl.when(up_from_here(slot))
+        def _():
+            up_pass(slot).wait_send()
 
     @pl.loop(1, n)
     def _(i):
@@ -662,7 +701,7 @@
     sine = jnp.concatenate([-sine, sine], axis=1)
     up = adapter_up_factors.T.reshape(pieces, chunk, LANES)
 
-    part_rows = STEPS * (heads_here + 4)
+    part_rows = up_to(STEPS * (heads_here + 4), 16)
     proj_rows = up_to(STEPS * heads_here, 16)
     soft_rows = 32 + 8
     out_rows = STEPS * (blocks + 1)
@@ -688,8 +727,8 @@
             pltpu.VMEM((2 * n, x_tall, LANES), bf16),
             pltpu.VMEM((2 * n, x_tall, LANES), bf16),
             pltpu.VMEM((x_tall, LANES), f32),
-            pltpu.VMEM((n, part_rows, LANES), f32),
-            pltpu.VMEM((n, part_rows, LANES), f32),
+            pltpu.VMEM((n, part_rows, LANES), bf16),
+            pltpu.VMEM((n, part_rows, LANES), bf16),
             pltpu.VMEM((proj_rows, LANES), bf16),
             pltpu.VMEM((n, proj_rows, LANES), bf16),
             pltpu.VMEM((n, STEPS * heads_here, LANES), f32),
@@ -702,7 +741,7 @@
             dma((7,)),
             dma((2 * n,)),
             dma((2 * n,)),
-            dma((pieces, 2)),
+            dma((pieces,)),
             dma((slots_up,)),
             dma((slots_up,)),
         ]

time: 55.9 us -> 49.1 us (0.88)
  Pallas kernels: 51.3 us -> 44.5 us
    pallas_call x1, Pallas kernels: 51.3 us -> 44.5 us  [fused(): pl.pallas_call(lambda *refs: fused_kernel(n, chunk, *refs), out_shape=jax...]
where the time goes in v3:
time: 49.1 us; the launch traced here: 48.8 us
  Pallas kernels  44.5 us (91%)
  local copies, waits for them, and re-layouts  2.81 us (6%)
  other arithmetic  0.81 us (2%)
  between operations  0.68 us (1%)
    pallas_call x1, Pallas kernels, fused(): pl.pallas_call(lambda *refs: fused_kernel(n, chunk, *refs), out_shape=jax...  44.5 us
    reshape x1, local copies, waits for them, and re-layouts, fused(): input_norm_gain.reshape(1, model_width)  1.32 us

profile of v3, /device:TPU:0, one launch (start us, length us, event | category | flops | bytes accessed | tf_op | source)
XLA Modules:
  0.0 48.8 jit_solution(15747502239062571750)
XLA Ops:
  0.7 0.1 fusion
  0.8 0.7 %pad_maximum_fusion = (f32[8,128]{1,0:T(8,128)}, f32[8,128]{1,0:T(8,128)}) fusion(f32[8,64]{1,0:T(8,128)S(1)} %get-tuple-element.7, f32[8,64]{1,0:T(8,128)S(1)} %get-tuple-element.6, f32[8,64]{1,0:T(8,128)S(1)} %get-tuple-element.5), kind=kLoop, calls=%fused_computation.2 | loop fusion | flops 2048 | bytes 14336 | tf_op jit(solution)/shard_map/concatenate | solution.py:700
  1.5 1.3 %reshape.30.refs_2_ = bf16[1,5120]{1,0:T(2,128)(2,1)} reshape(bf16[5120]{0:T(1024)(128)(2,1)} %param.15) | data formatting | bytes 20480 | tf_op jit(solution)/shard_map/reshape | solution.py:755
  2.8 44.5 %shard_map.109 = bf16[8,32,128]{2,1,0:T(8,128)(2,1)} custom-call(s32[2,4]{1,0:T(2,128)} %refs_0_.1, s32[1]{0:T(128)} %copy.15.refs_1_, bf16[1,5120]{1,0:T(2,128)(2,1)} %reshape.30.refs_2_, f32[8,128]{1,0:T(8,128)} %get-tuple-element.8.refs_3_, f32[8,128]{1,0:T(8,128)} %get-tuple-element.9.refs_4_, f32[2,128]{1,0:T(2,128)} %refs_5_.1, ...), custom_call_target="tpu_custom_call" | custom-call | tf_op jit(solution)/shard_map/pallas_call | solution.py:713
  47.3 0.8 %slice.3 = bf16[8,20,128]{2,1,0:T(8,128)(2,1)S(1)} slice(bf16[8,32,128]{2,1,0:T(8,128)(2,1)} %shard_map.109), slice={[0:8], [0:20], [0:128]} | slice | bytes 81920 | tf_op jit(solution)/shard_map/slice | solution.py:767
  48.1 0.7 %reshape.33 = bf16[1,4,5120]{2,1,0:T(4,128)(2,1)} reshape(bf16[4,8,5,128]{3,2,1,0:T(8,128)(2,1)S(1)} %copy.14) | data formatting | bytes 81920 | tf_op jit(solution)/shard_map/reshape | solution.py:768
  (4 shorter events, 0.1 us)

commit v4 on v3

--- a/solution.py
+++ b/solution.py
@@ -524,7 +524,12 @@
     diagonal = lax.broadcasted_iota(jnp.int32, (fine, LANES), 0) == lax.broadcasted_iota(
         jnp.int32, (fine, LANES), 1
     )
-    top_row = lax.broadcasted_iota(jnp.int32, (8, LANES), 0) == 0
+    stat_row = lax.broadcasted_iota(jnp.int32, (16, LANES), 0)
+
+    def three(row):
+        high = row.astype(jnp.bfloat16).astype(f32)
+        middle = (row - high).astype(jnp.bfloat16).astype(f32)
+        return high, middle, row - high - middle
 
     def to_row(column):
         return jnp.sum(jnp.where(diagonal, column, 0.0), axis=0, keepdims=True)
@@ -544,8 +549,11 @@
         count = jnp.sum(weights, axis=1, keepdims=True)
         soft_send[g, :fine] = jnp.dot(
             weights.astype(jnp.bfloat16), values, preferred_element_type=f32
-        )
-        soft_send[g, fine:] = jnp.where(top_row, to_row(top), to_row(count))
+        ).astype(jnp.bfloat16)
+        stats = jnp.zeros((16, LANES), f32)
+        for k, line in enumerate(three(to_row(top)) + three(to_row(count))):
+            stats = jnp.where(stat_row == k, line, stats)
+        soft_send[g, fine:] = stats.astype(jnp.bfloat16)
 
         @pl.when(i < n - 1)
         def _():
@@ -566,7 +574,8 @@
         peers_copy(
             soft_send.at[source], soft_recv.at[source], soft_ssem, soft_rsem, source, source
         ).wait_recv()
-    tops = [to_column(soft_recv[i, fine : fine + 1]) for i in range(n)]
+    stats = [soft_recv[i, fine:].astype(f32) for i in range(n)]
+    tops = [to_column(s[0:1] + s[1:2] + s[2:3]) for s in stats]
     largest = fresh_top
     for top in tops:
         largest = jnp.maximum(largest, top)
@@ -575,8 +584,8 @@
     numerator = jnp.dot(weights.astype(jnp.bfloat16), new_values, preferred_element_type=f32)
     for i in range(n):
         factor = jnp.exp(tops[i] - largest)
-        denominator += factor * to_column(soft_recv[i, fine + 1 : fine + 2])
-        numerator += factor * soft_recv[i, :fine]
+        denominator += factor * to_column(stats[i][3:4] + stats[i][4:5] + stats[i][5:6])
+        numerator += factor * soft_recv[i, :fine].astype(f32)
     attended = flat(numerator / denominator, fine // STEPS).astype(jnp.bfloat16)
 
     loads[5].wait()
@@ -703,7 +712,7 @@
 
     part_rows = up_to(STEPS * (heads_here + 4), 16)
     proj_rows = up_to(STEPS * heads_here, 16)
-    soft_rows = 32 + 8
+    soft_rows = 32 + 16
     out_rows = STEPS * (blocks + 1)
     slots_up = (width + in_rows) // chunk
     vmem = pl.BlockSpec(memory_space=pltpu.VMEM)
@@ -733,8 +742,8 @@
             pltpu.VMEM((n, proj_rows, LANES), bf16),
             pltpu.VMEM((n, STEPS * heads_here, LANES), f32),
             pltpu.VMEM((STEPS * QUERY_HEADS, LANES), bf16),
-            pltpu.VMEM((n, soft_rows, LANES), f32),
-            pltpu.VMEM((n, soft_rows, LANES), f32),
+            pltpu.VMEM((n, soft_rows, LANES), bf16),
+            pltpu.VMEM((n, soft_rows, LANES), bf16),
             pltpu.VMEM((n, out_rows, LANES), f32),
             pltpu.VMEM((n, out_rows, LANES), f32),
             pltpu.VMEM((x_tall, LANES), bf16),

time: 49.1 us -> 48.7 us (level)
  no operation moved by 1% of the time
where the time goes in v4:
time: 48.7 us; the launch traced here: 48.5 us
  Pallas kernels  44.2 us (91%)
  local copies, waits for them, and re-layouts  2.81 us (6%)
  other arithmetic  0.81 us (2%)
  between operations  0.68 us (1%)
    pallas_call x1, Pallas kernels, fused(): pl.pallas_call(lambda *refs: fused_kernel(n, chunk, *refs), out_shape=jax...  44.2 us
    reshape x1, local copies, waits for them, and re-layouts, fused(): input_norm_gain.reshape(1, model_width)  1.32 us

profile of v4, /device:TPU:0, one launch (start us, length us, event | category | flops | bytes accessed | tf_op | source)
XLA Modules:
  0.0 48.5 jit_solution(6726367079427166418)
XLA Ops:
  0.7 0.1 fusion
  0.8 0.7 %pad_maximum_fusion = (f32[8,128]{1,0:T(8,128)}, f32[8,128]{1,0:T(8,128)}) fusion(f32[8,64]{1,0:T(8,128)S(1)} %get-tuple-element.7, f32[8,64]{1,0:T(8,128)S(1)} %get-tuple-element.6, f32[8,64]{1,0:T(8,128)S(1)} %get-tuple-element.5), kind=kLoop, calls=%fused_computation.2 | loop fusion | flops 2048 | bytes 14336 | tf_op jit(solution)/shard_map/concatenate | solution.py:709
  1.5 1.3 %reshape.30.refs_2_ = bf16[1,5120]{1,0:T(2,128)(2,1)} reshape(bf16[5120]{0:T(1024)(128)(2,1)} %param.15) | data formatting | bytes 20480 | tf_op jit(solution)/shard_map/reshape | solution.py:764
  2.8 44.2 %shard_map.109 = bf16[8,32,128]{2,1,0:T(8,128)(2,1)} custom-call(s32[2,4]{1,0:T(2,128)} %refs_0_.1, s32[1]{0:T(128)} %copy.15.refs_1_, bf16[1,5120]{1,0:T(2,128)(2,1)} %reshape.30.refs_2_, f32[8,128]{1,0:T(8,128)} %get-tuple-element.8.refs_3_, f32[8,128]{1,0:T(8,128)} %get-tuple-element.9.refs_4_, f32[2,128]{1,0:T(2,128)} %refs_5_.1, ...), custom_call_target="tpu_custom_call" | custom-call | tf_op jit(solution)/shard_map/pallas_call | solution.py:722
  47.0 0.8 %slice.3 = bf16[8,20,128]{2,1,0:T(8,128)(2,1)S(1)} slice(bf16[8,32,128]{2,1,0:T(8,128)(2,1)} %shard_map.109), slice={[0:8], [0:20], [0:128]} | slice | bytes 81920 | tf_op jit(solution)/shard_map/slice | solution.py:776
  47.8 0.7 %reshape.33 = bf16[1,4,5120]{2,1,0:T(4,128)(2,1)} reshape(bf16[4,8,5,128]{3,2,1,0:T(8,128)(2,1)S(1)} %copy.14) | data formatting | bytes 81920 | tf_op jit(solution)/shard_map/reshape | solution.py:777
  (4 shorter events, 0.1 us)
